TPU v7x, 32 devices: a whole 2x2x4 slice. The times are simulated.
32 devices in a mesh: ctx: 8 (over z, x), ch: 4 (over y, core).
Axes of the slice: x: 2, y: 2, z: 4, core: 2. Of those that a mesh axis runs over, the one named last changes fastest.
Arguments:
- q_conv: bfloat16 [1792, 4096], P('ctx', 'ch'), may hold values from -6 to 6
- k_conv: bfloat16 [1792, 4096], P('ctx', 'ch'), may hold values from -6 to 6
- v_conv: bfloat16 [1792, 4096], P('ctx', 'ch'), may hold values from -6 to 6
- conv_filter: bfloat16 [1792, 256], P('ctx', 'ch'), may hold values from -1 to 1
- q_attn: bfloat16 [1792, 4096], P('ctx', 'ch'), may hold values from -5 to 5
- k_attn: bfloat16 [1792, 4096], P('ctx', 'ch'), may hold values from -5 to 5
- v_attn: bfloat16 [1792, 4096], P('ctx', 'ch'), may hold values from -6 to 6
- w_conv_out: bfloat16 [4096, 4096], P('ch'), may hold values from -0.09375 to 0.09375
- w_attn_out: bfloat16 [4096, 4096], P('ch'), may hold values from -0.375 to 0.375
Outputs:
- layer_out: bfloat16 [1792, 4096], P(('ctx', 'ch'))
All inputs are finite; a program needn't handle non-finite values.
Results may differ from a plain program's by a relative error of at most 0.018.
Values may be sent and summed in bfloat16 or wider, within the bound.
A program may use at most 192 MiB of HBM per device.

v0:
```python
from functools import partial
import math

import jax
import jax.numpy as jnp
from jax import lax
from jax.experimental import pallas as pl
from jax.experimental.pallas import tpu as pltpu
from jax.sharding import PartitionSpec as P

HD = 128


two_pi = 2.0 * math.pi
neg_large = -1e30
highest = lax.Precision.HIGHEST


def angle_table(left_idx, right_idx, period):
    product = left_idx[:, None] * right_idx[None, :] % period
    return product.astype(jnp.float32) * (two_pi / period)


def section_coarse(values, cos_table, sin_table, twiddle):
    real_part = jnp.einsum("kn,nsc->ksc", cos_table, values, precision=highest)
    imag_part = -jnp.einsum("kn,nsc->ksc", sin_table, values, precision=highest)
    cos_twist = jnp.cos(twiddle)[:, :, None]
    sin_twist = jnp.sin(twiddle)[:, :, None]
    return (
        real_part * cos_twist + imag_part * sin_twist,
        imag_part * cos_twist - real_part * sin_twist,
    )


def section_fine(real_part, imag_part, cos_table, sin_table, direction):
    cos_real = jnp.einsum("kn,anc->akc", cos_table, real_part, precision=highest)
    cos_imag = jnp.einsum("kn,anc->akc", cos_table, imag_part, precision=highest)
    sin_real = jnp.einsum("kn,anc->akc", sin_table, real_part, precision=highest)
    sin_imag = jnp.einsum("kn,anc->akc", sin_table, imag_part, precision=highest)
    return (cos_real - direction * sin_imag, cos_imag + direction * sin_real)


def spectral_conv(gated, filters, my_index, tok_rows, count_ctx):
    chans = gated.shape[1]
    groups = filters.shape[1]
    share = chans // groups
    sub_rows = tok_rows // count_ctx
    period = 2 * count_ctx * tok_rows
    got_source, got_filter = (
        lax.all_to_all(
            gated.reshape(1, tok_rows, chans), "ctx", split_axis=1, concat_axis=0, tiled=True
        ),
        lax.all_to_all(
            filters.reshape(1, tok_rows, groups), "ctx", split_axis=1, concat_axis=0, tiled=True
        ),
    )
    coarse_idx = jnp.arange(count_ctx, dtype=jnp.int32)
    coarse_freq = jnp.arange(2 * count_ctx, dtype=jnp.int32)
    coarse_angle = angle_table(coarse_freq, coarse_idx, 2 * count_ctx)
    cos_coarse = jnp.cos(coarse_angle)
    sin_coarse = jnp.sin(coarse_angle)
    fine_global = my_index * sub_rows + jnp.arange(sub_rows, dtype=jnp.int32)
    twist_in = angle_table(coarse_freq, fine_global, period)
    source_re, source_im = section_coarse(
        got_source.astype(jnp.float32), cos_coarse, sin_coarse, twist_in
    )
    filter_re, filter_im = section_coarse(
        got_filter.astype(jnp.float32), cos_coarse, sin_coarse, twist_in
    )
    source_re, source_im, filter_re, filter_im = (
        lax.all_to_all(
            source_re.astype(jnp.bfloat16), "ctx", split_axis=0, concat_axis=1, tiled=True
        ).astype(source_re.dtype),
        lax.all_to_all(
            source_im.astype(jnp.bfloat16), "ctx", split_axis=0, concat_axis=1, tiled=True
        ).astype(source_im.dtype),
        lax.all_to_all(
            filter_re.astype(jnp.bfloat16), "ctx", split_axis=0, concat_axis=1, tiled=True
        ).astype(filter_re.dtype),
        lax.all_to_all(
            filter_im.astype(jnp.bfloat16), "ctx", split_axis=0, concat_axis=1, tiled=True
        ).astype(filter_im.dtype),
    )
    fine_idx = jnp.arange(tok_rows, dtype=jnp.int32)
    fine_angle = angle_table(fine_idx, fine_idx, tok_rows)
    cos_fine = jnp.cos(fine_angle)
    sin_fine = jnp.sin(fine_angle)
    source_re, source_im = section_fine(source_re, source_im, cos_fine, sin_fine, -1.0)
    filter_re, filter_im = section_fine(filter_re, filter_im, cos_fine, sin_fine, -1.0)
    split_re = source_re.reshape(2, tok_rows, groups, share)
    split_im = source_im.reshape(2, tok_rows, groups, share)
    prod_re = split_re * filter_re[..., None] - split_im * filter_im[..., None]
    prod_im = split_re * filter_im[..., None] + split_im * filter_re[..., None]
    back_re, back_im = section_fine(
        prod_re.reshape(2, tok_rows, chans),
        prod_im.reshape(2, tok_rows, chans),
        cos_fine,
        sin_fine,
        1.0,
    )
    pair_freq = my_index * 2 + jnp.arange(2, dtype=jnp.int32)
    twist_out = angle_table(pair_freq, fine_idx, period)
    cos_out = jnp.cos(twist_out)[:, :, None]
    sin_out = jnp.sin(twist_out)[:, :, None]
    turned_re = back_re * cos_out - back_im * sin_out
    turned_im = back_re * sin_out + back_im * cos_out
    turned_re, turned_im = (
        lax.all_to_all(
            turned_re.astype(jnp.bfloat16), "ctx", split_axis=1, concat_axis=0, tiled=True
        ).astype(turned_re.dtype),
        lax.all_to_all(
            turned_im.astype(jnp.bfloat16), "ctx", split_axis=1, concat_axis=0, tiled=True
        ).astype(turned_im.dtype),
    )
    result = jnp.einsum("nk,ksc->nsc", cos_coarse.T, turned_re, precision=highest)
    result = result - jnp.einsum("nk,ksc->nsc", sin_coarse.T, turned_im, precision=highest)
    rounded = (result / period).astype(jnp.bfloat16)
    returned = lax.all_to_all(rounded, "ctx", split_axis=0, concat_axis=1, tiled=True)
    return returned.reshape(tok_rows, chans)


def keep_same(running):
    return running


def attend_block(group_query, group_pos, key_block, value_block, key_pos, score_scale, group_state):
    run_max, run_total, run_accum = group_state
    scores = (
        jnp.einsum("thd,shd->hts", group_query, key_block, preferred_element_type=jnp.float32)
        * score_scale
    )
    allowed = (key_pos[None, :] <= group_pos[:, None])[None]
    block_max = jnp.max(jnp.where(allowed, scores, neg_large), axis=2)
    new_max = jnp.maximum(run_max, block_max)
    factor = jnp.exp(run_max - new_max)
    weights = jnp.where(allowed, jnp.exp(scores - new_max[:, :, None]), 0.0)
    new_total = run_total * factor + jnp.sum(weights, axis=2)
    new_accum = run_accum * factor[:, :, None] + jnp.einsum(
        "hts,shd->htd",
        weights.astype(jnp.bfloat16),
        value_block,
        preferred_element_type=jnp.float32,
    )
    return (new_max, new_total, new_accum)


def attention(q_attn, k_attn, v_attn, my_index, tok_rows):
    heads_local = q_attn.shape[1] // HD
    score_scale = HD ** (-0.5)
    queries = q_attn.reshape(tok_rows, heads_local, HD)
    group_list = [(queries, my_index * tok_rows + jnp.arange(tok_rows, dtype=jnp.int32))]
    initial = tuple(
        (
            (
                jnp.full((heads_local, entry[0].shape[0]), neg_large, jnp.float32),
                jnp.zeros((heads_local, entry[0].shape[0]), jnp.float32),
                jnp.zeros((heads_local, entry[0].shape[0], HD), jnp.float32),
            )
            for entry in group_list
        )
    )
    key_piece = lax.all_gather(k_attn, "ctx", axis=0, tiled=True)
    value_piece = lax.all_gather(v_attn, "ctx", axis=0, tiled=True)
    count_blocks = key_piece.shape[0] // tok_rows
    keys_split = key_piece.reshape(count_blocks, tok_rows, heads_local, HD)
    values_split = value_piece.reshape(count_blocks, tok_rows, heads_local, HD)

    def one_block(carry, item):
        key_block, value_block, block_number = item
        block_first = block_number * tok_rows
        key_pos = block_first + jnp.arange(tok_rows, dtype=jnp.int32)
        updated = []
        for entry, group_state in zip(group_list, carry):
            step_fn = partial(
                attend_block, entry[0], entry[1], key_block, value_block, key_pos, score_scale
            )
            updated.append(lax.cond(block_first <= entry[1][-1], step_fn, keep_same, group_state))
        return (tuple(updated), None)

    new_state, unused = lax.scan(
        one_block, initial, (keys_split, values_split, jnp.arange(count_blocks, dtype=jnp.int32))
    )
    outputs = [
        (state[2] / state[1][:, :, None]).transpose(1, 0, 2).astype(jnp.bfloat16)
        for state in new_state
    ]
    merged = outputs[0]
    return merged.reshape(tok_rows, heads_local * HD)


def local_general(q_conv, k_conv, v_conv, conv_filter, q_attn, k_attn, v_attn, w_conv_out, w_attn_out):
    count_ctx = lax.axis_size("ctx")
    my_index = lax.axis_index("ctx")
    tok_rows = q_conv.shape[0]
    gated = (k_conv.astype(jnp.float32) * v_conv.astype(jnp.float32)).astype(jnp.bfloat16)
    conv = spectral_conv(gated, conv_filter, my_index, tok_rows, count_ctx)
    mixed = (q_conv.astype(jnp.float32) * conv.astype(jnp.float32)).astype(jnp.bfloat16)
    attended = attention(q_attn, k_attn, v_attn, my_index, tok_rows)
    return lax.psum_scatter(
        (
            jnp.dot(mixed, w_conv_out, preferred_element_type=jnp.float32)
            + jnp.dot(attended, w_attn_out, preferred_element_type=jnp.float32)
        ).astype(jnp.bfloat16),
        "ch",
        scatter_dimension=0,
        tiled=True,
    )


GROUP = 16
TILE = 256
HALF = 128
MESH = pl.DeviceIdType.MESH


def fused_kernel(
    count_ctx, rows, width,
    qc_ref, kc_ref, vc_ref, filt_ref, q_ref, k_ref, v_ref, w1_hbm, w2_hbm,
    out_ref,
    gated, filt_in, gated_in, q_in, k_in, v_in, conv_out, attn_out, conv_back, attn_back,
    fpad, x_turned, y_turned, stage, lhs_conv, lhs_attn, w1, w2,
    keep, send_a, recv_a, send_b, recv_b,
    in_send, in_recv, back_send, back_recv, w_sem, a_send, a_recv, b_send, b_recv,
):
    me = lax.axis_index("ctx")
    ch = lax.axis_index("ch")
    core = lax.rem(ch, 2)
    pair = ch // 2
    core_peer = pair * 2 + (1 - core)
    pair_peer = (1 - pair) * 2 + core
    tokens = count_ctx * rows
    tiles = tokens // TILE
    groups = HD // GROUP

    w1_copy = pltpu.make_async_copy(w1_hbm, w1, w_sem.at[0])
    w2_copy = pltpu.make_async_copy(w2_hbm, w2, w_sem.at[1])
    w1_copy.start()
    w2_copy.start()

    barrier = pltpu.get_barrier_semaphore()
    for k in range(1, count_ctx):
        peer = lax.rem(me + k, count_ctx)
        pl.semaphore_signal(barrier, inc=1, device_id=(peer, ch), device_id_type=MESH)
    pl.semaphore_signal(barrier, inc=1, device_id=(me, core_peer), device_id_type=MESH)
    pl.semaphore_signal(barrier, inc=1, device_id=(me, pair_peer), device_id_type=MESH)

    gated[...] = (kc_ref[...].astype(jnp.float32) * vc_ref[...].astype(jnp.float32)).astype(
        jnp.bfloat16
    )
    pl.semaphore_wait(barrier, count_ctx + 1)

    my_rows = pl.ds(pl.multiple_of(me * rows, 16), rows)
    my_cols = pl.ds(pl.multiple_of(me * HD, HD), HD)
    my_groups = pl.ds(pl.multiple_of(me * groups, groups), groups)
    pieces = ((gated, gated_in), (q_ref, q_in), (k_ref, k_in), (v_ref, v_in))
    inbound = [[] for unused in range(5)]
    for k in range(1, count_ctx):
        peer = lax.rem(me + k, count_ctx)
        peer_groups = pl.ds(pl.multiple_of(peer * groups, groups), groups)
        copy = pltpu.make_async_remote_copy(
            src_ref=filt_ref.at[peer_groups, :],
            dst_ref=filt_in.at[me],
            send_sem=in_send.at[4, k],
            recv_sem=in_recv.at[4, k],
            device_id=(peer, ch),
            device_id_type=MESH,
        )
        copy.start()
        inbound[4].append(copy)
    for number, (source, target) in enumerate(pieces):
        for k in range(1, count_ctx):
            peer = lax.rem(me + k, count_ctx)
            peer_cols = pl.ds(pl.multiple_of(peer * HD, HD), HD)
            copy = pltpu.make_async_remote_copy(
                src_ref=source.at[:, peer_cols],
                dst_ref=target.at[my_rows, :],
                send_sem=in_send.at[number, k],
                recv_sem=in_recv.at[number, k],
                device_id=(peer, ch),
                device_id_type=MESH,
            )
            copy.start()
            inbound[number].append(copy)
    for source, target in pieces:
        target[my_rows, :] = source[:, my_cols]
    filt_in[pl.ds(me, 1)] = filt_ref[my_groups, :].reshape(1, groups, filt_ref.shape[1])

    def send_back(source, target, number):
        copies = []
        for k in range(1, count_ctx):
            peer = lax.rem(me + k, count_ctx)
            peer_rows = pl.ds(pl.multiple_of(peer * rows, 16), rows)
            copy = pltpu.make_async_remote_copy(
                src_ref=source.at[peer_rows, :],
                dst_ref=target.at[:, my_cols],
                send_sem=back_send.at[number, k],
                recv_sem=back_recv.at[number, k],
                device_id=(peer, ch),
                device_id_type=MESH,
            )
            copy.start()
            copies.append(copy)
        target[:, my_cols] = source[my_rows, :]
        return copies

    for copy in inbound[4]:
        copy.wait_recv()
    fpad[...] = jnp.zeros_like(fpad)
    wide = filt_ref.shape[1]
    for j in range(count_ctx):
        first = HALF + j * rows
        base = first // HALF * HALF
        piece = jnp.concatenate(
            [filt_in[j], jnp.zeros((groups, HALF), jnp.float32)], axis=1
        )
        if first % HALF:
            piece = pltpu.roll(piece, first % HALF, 1)
        fpad[:, base : base + wide + HALF] += piece

    for copy in inbound[0]:
        copy.wait_recv()
    for j in range(tiles):
        turned = (
            gated_in[j * TILE : (j + 1) * TILE, :].astype(jnp.float32).T.astype(jnp.bfloat16)
        )
        for g in range(groups):
            x_turned[g, j * GROUP : (j + 1) * GROUP, :] = turned[g * GROUP : (g + 1) * GROUP, :]

    span = tokens + HALF

    def one_group(g, carry):
        line = fpad[pl.ds(g, 1), 0 : span + HALF]
        shifted = pltpu.roll(
            jnp.broadcast_to(line, (HALF, span + HALF)), 0, 1, stride=1, stride_axis=0
        ).astype(jnp.bfloat16)
        for d in range(tiles):
            block = jnp.concatenate(
                [
                    shifted[:, HALF + d * TILE : HALF + (d + 1) * TILE],
                    shifted[:, d * TILE : (d + 1) * TILE],
                ],
                axis=0,
            )
            part = jnp.dot(
                x_turned[g, 0 : (tiles - d) * GROUP, :], block, preferred_element_type=jnp.float32
            )
            if d == 0:
                y_turned[g] = part
            else:
                y_turned[g, d * GROUP :, :] += part
        return carry

    lax.fori_loop(0, groups, one_group, 0)
    for i in range(tiles):
        gathered = y_turned[:, i * GROUP : (i + 1) * GROUP, :].reshape(HD, TILE)
        conv_out[i * TILE : (i + 1) * TILE, :] = gathered.T.astype(jnp.bfloat16)
    conv_copies = send_back(conv_out, conv_back, 0)

    for number in (1, 2, 3):
        for copy in inbound[number]:
            copy.wait_recv()
    factor = HD ** (-0.5) * math.log2(math.e)
    below = lax.broadcasted_iota(jnp.int32, (TILE, TILE), 1) <= lax.broadcasted_iota(
        jnp.int32, (TILE, TILE), 0
    )
    for i in range(tiles):
        query = q_in[i * TILE : (i + 1) * TILE, :]
        scores = lax.dot_general(
            query,
            k_in[0 : (i + 1) * TILE, :],
            (((1,), (1,)), ((), ())),
            preferred_element_type=jnp.float32,
        )
        corner = jnp.where(below, scores[:, i * TILE :], neg_large)
        if i:
            scores = jnp.concatenate([scores[:, : i * TILE], corner], axis=1)
        else:
            scores = corner
        row_max = jnp.max(scores, axis=1, keepdims=True)
        weights = jnp.exp2((scores - row_max) * factor)
        totals = jnp.sum(weights, axis=1, keepdims=True)
        summed = jnp.dot(
            weights.astype(jnp.bfloat16),
            v_in[0 : (i + 1) * TILE, :],
            preferred_element_type=jnp.float32,
        )
        attn_out[i * TILE : (i + 1) * TILE, :] = (summed / totals).astype(jnp.bfloat16)
    attn_copies = send_back(attn_out, attn_back, 1)

    share = rows // 4
    padded = keep.shape[1] // 2
    order = (ch, pair_peer, core_peer, (1 - pair) * 2 + (1 - core))

    def place(target):
        for slot, owner in enumerate(order):
            part = stage[pl.ds(pl.multiple_of(owner * share, 8), share), :]
            filler = jnp.zeros((padded - share, width), jnp.float32)
            target[slot * padded : (slot + 1) * padded, :] = jnp.concatenate(
                [part, filler], axis=0
            ).astype(jnp.bfloat16)

    for copy in conv_copies:
        copy.wait_recv()
    stage[...] = qc_ref[...].astype(jnp.float32) * conv_back[...].astype(jnp.float32)
    place(lhs_conv)
    w1_copy.wait()
    w2_copy.wait()
    for copy in attn_copies:
        copy.wait_recv()
    stage[...] = attn_back[...].astype(jnp.float32)
    place(lhs_attn)

    chunks, unused, chunk = keep.shape

    def copy_a(n):
        return pltpu.make_async_remote_copy(
            src_ref=send_a.at[n],
            dst_ref=recv_a.at[n],
            send_sem=a_send.at[n],
            recv_sem=a_recv.at[n],
            device_id=(me, core_peer),
            device_id_type=MESH,
        )

    def copy_b(n):
        return pltpu.make_async_remote_copy(
            src_ref=send_b.at[n],
            dst_ref=recv_b.at[n],
            send_sem=b_send.at[n],
            recv_sem=b_recv.at[n],
            device_id=(me, pair_peer),
            device_id_type=MESH,
        )

    def project(n):
        cols = pl.ds(pl.multiple_of(n * chunk, chunk), chunk)
        total = jnp.dot(
            lhs_conv[...], w1[:, cols], preferred_element_type=jnp.float32
        ) + jnp.dot(lhs_attn[...], w2[:, cols], preferred_element_type=jnp.float32)
        keep[n] = total[0 : 2 * padded]
        send_a[n] = total[2 * padded :].astype(jnp.bfloat16)
        copy_a(n).start()

    def forward(n):
        copy_a(n).wait_recv()
        send_b[n] = (
            keep[n, padded:, :] + recv_a[n, padded:, :].astype(jnp.float32)
        ).astype(jnp.bfloat16)
        copy_b(n).start()

    project(0)

    def one_chunk(n, carry):
        project(n)
        forward(n - 1)
        return carry

    lax.fori_loop(1, chunks, one_chunk, 0)
    forward(chunks - 1)

    def finish(n, carry):
        cols = pl.ds(pl.multiple_of(n * chunk, chunk), chunk)
        copy_b(n).wait_recv()
        total = (
            keep[n, 0:padded, :]
            + recv_a[n, 0:padded, :].astype(jnp.float32)
            + recv_b[n].astype(jnp.float32)
        )
        out_ref[:, cols] = total[0:share].astype(jnp.bfloat16)
        copy_a(n).wait_send()
        copy_b(n).wait_send()
        return carry

    lax.fori_loop(0, chunks, finish, 0)
    for copies in inbound + [conv_copies, attn_copies]:
        for copy in copies:
            copy.wait_send()


def local_fused(q_conv, k_conv, v_conv, conv_filter, q_attn, k_attn, v_attn, w_conv_out, w_attn_out):
    count_ctx = lax.axis_size("ctx")
    rows, width = q_conv.shape
    dout = w_conv_out.shape[1]
    tokens = count_ctx * rows
    groups = HD // GROUP
    wide = (rows + HALF - 1) // HALF * HALF
    filt = jnp.pad(conv_filter.T.astype(jnp.float32), ((0, 0), (0, wide - rows)))
    share = rows // 4
    padded = (share + 15) // 16 * 16
    chunk = 512
    chunks = dout // chunk
    tiles = tokens // TILE
    bf16, f32 = jnp.bfloat16, jnp.float32
    vmem = pl.BlockSpec(memory_space=pltpu.VMEM)
    hbm = pl.BlockSpec(memory_space=pl.ANY)
    dma = pltpu.SemaphoreType.DMA
    return pl.pallas_call(
        partial(fused_kernel, count_ctx, rows, width),
        out_shape=jax.ShapeDtypeStruct((share, dout), bf16),
        in_specs=[vmem] * 7 + [hbm] * 2,
        out_specs=vmem,
        scratch_shapes=[
            pltpu.VMEM((rows, width), bf16),
            pltpu.VMEM((count_ctx, groups, wide), f32),
            pltpu.VMEM((tokens, HD), bf16),
            pltpu.VMEM((tokens, HD), bf16),
            pltpu.VMEM((tokens, HD), bf16),
            pltpu.VMEM((tokens, HD), bf16),
            pltpu.VMEM((tokens, HD), bf16),
            pltpu.VMEM((tokens, HD), bf16),
            pltpu.VMEM((rows, width), bf16),
            pltpu.VMEM((rows, width), bf16),
            pltpu.VMEM((groups, tokens + 2 * HALF + TILE), f32),
            pltpu.VMEM((groups, tiles * GROUP, TILE), bf16),
            pltpu.VMEM((groups, tiles * GROUP, TILE), f32),
            pltpu.VMEM((rows, width), f32),
            pltpu.VMEM((4 * padded, width), bf16),
            pltpu.VMEM((4 * padded, width), bf16),
            pltpu.VMEM(w_conv_out.shape, bf16),
            pltpu.VMEM(w_attn_out.shape, bf16),
            pltpu.VMEM((chunks, 2 * padded, chunk), f32),
            pltpu.VMEM((chunks, 2 * padded, chunk), bf16),
            pltpu.VMEM((chunks, 2 * padded, chunk), bf16),
            pltpu.VMEM((chunks, padded, chunk), bf16),
            pltpu.VMEM((chunks, padded, chunk), bf16),
            dma((5, count_ctx)),
            dma((5, count_ctx)),
            dma((2, count_ctx)),
            dma((2, count_ctx)),
            dma((2,)),
            dma((chunks,)),
            dma((chunks,)),
            dma((chunks,)),
            dma((chunks,)),
        ],
        compiler_params=pltpu.CompilerParams(
            collective_id=0, has_side_effects=True, vmem_limit_bytes=56 * 1024 * 1024
        ),
        name="fused_block",
    )(q_conv, k_conv, v_conv, filt, q_attn, k_attn, v_attn, w_conv_out, w_attn_out)


def local(q_conv, k_conv, v_conv, conv_filter, q_attn, k_attn, v_attn, w_conv_out, w_attn_out):
    count_ctx = lax.axis_size("ctx")
    rows, width = q_conv.shape
    dout = w_conv_out.shape[1]
    fits = (
        width == count_ctx * HD
        and conv_filter.shape[1] * GROUP == width
        and lax.axis_size("ch") == 4
        and rows % 32 == 0
        and (count_ctx * rows) % TILE == 0
        and count_ctx * rows <= 2048
        and dout % 512 == 0
    )
    chosen = local_fused if fits else local_general
    return chosen(
        q_conv, k_conv, v_conv, conv_filter, q_attn, k_attn, v_attn, w_conv_out, w_attn_out
    )


def solution(mesh):
    return jax.shard_map(
        local,
        mesh=mesh,
        in_specs=(
            P("ctx", "ch"),
            P("ctx", "ch"),
            P("ctx", "ch"),
            P("ctx", "ch"),
            P("ctx", "ch"),
            P("ctx", "ch"),
            P("ctx", "ch"),
            P("ch", None),
            P("ch", None),
        ),
        out_specs=P(("ctx", "ch"), None),
        check_vma=False,
    )
```

profile of v0, /device:TPU:0, one launch (start us, length us, event | category | flops | bytes accessed | tf_op | source)
XLA Modules:
  0.0 86.8 jit_solution(16656281747902424636)
XLA Ops:
  0.0 1.4 %pad_convert_fusion.filt_ref = f32[64,256]{1,0:T(8,128)} fusion(bf16[64,224]{1,0:T(8,128)(2,1)} %bitcast.1), kind=kLoop, calls=%fused_computation | loop fusion | flops 16384 | bytes 94208 | tf_op jit(solution)/shard_map/jit(_pad)/pad | solution.py:487
  1.4 83.6 %fused_block.1 = bf16[56,4096]{1,0:T(8,128)(2,1)} custom-call(bf16[224,1024]{1,0:T(8,128)(2,1)} %qc_ref.1, bf16[224,1024]{1,0:T(8,128)(2,1)} %kc_ref.1, bf16[224,1024]{1,0:T(8,128)(2,1)} %vc_ref.1, f32[64,256]{1,0:T(8,128)} %pad_convert_fusion.filt_ref, bf16[224,1024]{1,0:T(8,128)(2,1)} %q_ref.1, bf16[224,1024]{1,0:T(8,128)(2,1)} %k_ref.1, ...), custom_call_target="tpu_custom_call" | custom-call | tf_op jit(solution)/shard_map/fused_block/pallas_call | solution.py:497
  85.0 1.8 %copy.11 = bf16[56,4096]{1,0:T(8,128)(2,1)} copy(bf16[56,4096]{1,0:T(8,128)(2,1)} %fused_block.1) | data formatting | bytes 917504
where the time goes:
time: 88.3 us; the launch traced here: 86.8 us
  Pallas kernels  83.6 us (95%)
  local copies, waits for them, and re-layouts  1.82 us (2%)
  other arithmetic  1.39 us (2%)
    pallas_call x1, Pallas kernels, local_fused(): pl.pallas_call(partial(fused_kernel, count_ctx, rows, width), out_shape=j...  83.6 us
    unnamed x1, local copies, waits for them, and re-layouts  1.82 us

commit v1 on v0

--- a/solution.py
+++ b/solution.py
@@ -215,12 +215,13 @@
 
 def fused_kernel(
     count_ctx, rows, width,
-    qc_ref, kc_ref, vc_ref, filt_ref, q_ref, k_ref, v_ref, w1_hbm, w2_hbm,
+    qc_hbm, kc_hbm, vc_hbm, filt_ref, q_ref, k_ref, v_ref, w1_hbm, w2_hbm,
     out_ref,
+    qc, kc, vc, filt,
     gated, filt_in, gated_in, q_in, k_in, v_in, conv_out, attn_out, conv_back, attn_back,
     fpad, x_turned, y_turned, stage, lhs_conv, lhs_attn, w1, w2,
     keep, send_a, recv_a, send_b, recv_b,
-    in_send, in_recv, back_send, back_recv, w_sem, a_send, a_recv, b_send, b_recv,
+    in_send, in_recv, back_send, back_recv, load_sem, a_send, a_recv, b_send, b_recv,
 ):
     me = lax.axis_index("ctx")
     ch = lax.axis_index("ch")
@@ -231,11 +232,9 @@
     tokens = count_ctx * rows
     tiles = tokens // TILE
     groups = HD // GROUP
-
-    w1_copy = pltpu.make_async_copy(w1_hbm, w1, w_sem.at[0])
-    w2_copy = pltpu.make_async_copy(w2_hbm, w2, w_sem.at[1])
-    w1_copy.start()
-    w2_copy.start()
+    my_rows = pl.ds(pl.multiple_of(me * rows, 16), rows)
+    my_cols = pl.ds(pl.multiple_of(me * HD, HD), HD)
+    my_groups = pl.ds(pl.multiple_of(me * groups, groups), groups)
 
     barrier = pltpu.get_barrier_semaphore()
     for k in range(1, count_ctx):
@@ -244,30 +243,25 @@
     pl.semaphore_signal(barrier, inc=1, device_id=(me, core_peer), device_id_type=MESH)
     pl.semaphore_signal(barrier, inc=1, device_id=(me, pair_peer), device_id_type=MESH)
 
-    gated[...] = (kc_ref[...].astype(jnp.float32) * vc_ref[...].astype(jnp.float32)).astype(
-        jnp.bfloat16
-    )
+    heads = ((q_ref, q_in), (k_ref, k_in), (v_ref, v_in))
+    kc_copy = pltpu.make_async_copy(kc_hbm, kc, load_sem.at[0])
+    vc_copy = pltpu.make_async_copy(vc_hbm, vc, load_sem.at[1])
+    own_copies = [
+        pltpu.make_async_copy(source.at[:, my_cols], target.at[my_rows, :], load_sem.at[2 + n])
+        for n, (source, target) in enumerate(heads)
+    ]
+    qc_copy = pltpu.make_async_copy(qc_hbm, qc, load_sem.at[5])
+    w1_copy = pltpu.make_async_copy(w1_hbm, w1, load_sem.at[6])
+    w2_copy = pltpu.make_async_copy(w2_hbm, w2, load_sem.at[7])
+    kc_copy.start()
+    vc_copy.start()
+    filt[...] = jnp.zeros_like(filt)
+    filt[:, 0:rows] = filt_ref[...].astype(jnp.float32)
     pl.semaphore_wait(barrier, count_ctx + 1)
 
-    my_rows = pl.ds(pl.multiple_of(me * rows, 16), rows)
-    my_cols = pl.ds(pl.multiple_of(me * HD, HD), HD)
-    my_groups = pl.ds(pl.multiple_of(me * groups, groups), groups)
-    pieces = ((gated, gated_in), (q_ref, q_in), (k_ref, k_in), (v_ref, v_in))
     inbound = [[] for unused in range(5)]
-    for k in range(1, count_ctx):
-        peer = lax.rem(me + k, count_ctx)
-        peer_groups = pl.ds(pl.multiple_of(peer * groups, groups), groups)
-        copy = pltpu.make_async_remote_copy(
-            src_ref=filt_ref.at[peer_groups, :],
-            dst_ref=filt_in.at[me],
-            send_sem=in_send.at[4, k],
-            recv_sem=in_recv.at[4, k],
-            device_id=(peer, ch),
-            device_id_type=MESH,
-        )
-        copy.start()
-        inbound[4].append(copy)
-    for number, (source, target) in enumerate(pieces):
+
+    def spread(source, target, number):
         for k in range(1, count_ctx):
             peer = lax.rem(me + k, count_ctx)
             peer_cols = pl.ds(pl.multiple_of(peer * HD, HD), HD)
@@ -281,18 +275,40 @@
             )
             copy.start()
             inbound[number].append(copy)
-    for source, target in pieces:
-        target[my_rows, :] = source[:, my_cols]
-    filt_in[pl.ds(me, 1)] = filt_ref[my_groups, :].reshape(1, groups, filt_ref.shape[1])
-
-    def send_back(source, target, number):
+
+    for k in range(1, count_ctx):
+        peer = lax.rem(me + k, count_ctx)
+        peer_groups = pl.ds(pl.multiple_of(peer * groups, groups), groups)
+        copy = pltpu.make_async_remote_copy(
+            src_ref=filt.at[peer_groups, :],
+            dst_ref=filt_in.at[me],
+            send_sem=in_send.at[4, k],
+            recv_sem=in_recv.at[4, k],
+            device_id=(peer, ch),
+            device_id_type=MESH,
+        )
+        copy.start()
+        inbound[4].append(copy)
+    for number, (source, target) in enumerate(heads):
+        spread(source, target, number + 1)
+    for copy in own_copies + [qc_copy, w1_copy, w2_copy]:
+        copy.start()
+    kc_copy.wait()
+    vc_copy.wait()
+    gated[...] = (kc[...].astype(jnp.float32) * vc[...].astype(jnp.float32)).astype(jnp.bfloat16)
+    spread(gated, gated_in, 0)
+    gated_in[my_rows, :] = gated[:, my_cols]
+    filt_in[pl.ds(me, 1)] = filt[my_groups, :].reshape(1, groups, filt.shape[1])
+
+    def send_back(source, target, number, first, count):
         copies = []
+        here = pl.ds(pl.multiple_of(first, 16), count)
         for k in range(1, count_ctx):
             peer = lax.rem(me + k, count_ctx)
-            peer_rows = pl.ds(pl.multiple_of(peer * rows, 16), rows)
+            peer_rows = pl.ds(pl.multiple_of(peer * rows + first, 16), count)
             copy = pltpu.make_async_remote_copy(
                 src_ref=source.at[peer_rows, :],
-                dst_ref=target.at[:, my_cols],
+                dst_ref=target.at[here, my_cols],
                 send_sem=back_send.at[number, k],
                 recv_sem=back_recv.at[number, k],
                 device_id=(peer, ch),
@@ -300,13 +316,47 @@
             )
             copy.start()
             copies.append(copy)
-        target[:, my_cols] = source[my_rows, :]
+        kept_rows = pl.ds(pl.multiple_of(me * rows + first, 16), count)
+        target[here, my_cols] = source[kept_rows, :]
         return copies
+
+    for copy in own_copies:
+        copy.wait()
+    for number in (1, 2, 3):
+        for copy in inbound[number]:
+            copy.wait_recv()
+    factor = HD ** (-0.5) * math.log2(math.e)
+    below = lax.broadcasted_iota(jnp.int32, (TILE, TILE), 1) <= lax.broadcasted_iota(
+        jnp.int32, (TILE, TILE), 0
+    )
+    for i in range(tiles):
+        query = q_in[i * TILE : (i + 1) * TILE, :]
+        scores = lax.dot_general(
+            query,
+            k_in[0 : (i + 1) * TILE, :],
+            (((1,), (1,)), ((), ())),
+            preferred_element_type=jnp.float32,
+        )
+        corner = jnp.where(below, scores[:, i * TILE :], neg_large)
+        if i:
+            scores = jnp.concatenate([scores[:, : i * TILE], corner], axis=1)
+        else:
+            scores = corner
+        row_max = jnp.max(scores, axis=1, keepdims=True)
+        weights = jnp.exp2((scores - row_max) * factor)
+        totals = jnp.sum(weights, axis=1, keepdims=True)
+        summed = jnp.dot(
+            weights.astype(jnp.bfloat16),
+            v_in[0 : (i + 1) * TILE, :],
+            preferred_element_type=jnp.float32,
+        )
+        attn_out[i * TILE : (i + 1) * TILE, :] = (summed / totals).astype(jnp.bfloat16)
+    attn_copies = send_back(attn_out, attn_back, 0, 0, rows)
 
     for copy in inbound[4]:
         copy.wait_recv()
     fpad[...] = jnp.zeros_like(fpad)
-    wide = filt_ref.shape[1]
+    wide = filt.shape[1]
     for j in range(count_ctx):
         first = HALF + j * rows
         base = first // HALF * HALF
@@ -354,63 +404,31 @@
     for i in range(tiles):
         gathered = y_turned[:, i * GROUP : (i + 1) * GROUP, :].reshape(HD, TILE)
         conv_out[i * TILE : (i + 1) * TILE, :] = gathered.T.astype(jnp.bfloat16)
-    conv_copies = send_back(conv_out, conv_back, 0)
-
-    for number in (1, 2, 3):
-        for copy in inbound[number]:
-            copy.wait_recv()
-    factor = HD ** (-0.5) * math.log2(math.e)
-    below = lax.broadcasted_iota(jnp.int32, (TILE, TILE), 1) <= lax.broadcasted_iota(
-        jnp.int32, (TILE, TILE), 0
-    )
-    for i in range(tiles):
-        query = q_in[i * TILE : (i + 1) * TILE, :]
-        scores = lax.dot_general(
-            query,
-            k_in[0 : (i + 1) * TILE, :],
-            (((1,), (1,)), ((), ())),
-            preferred_element_type=jnp.float32,
-        )
-        corner = jnp.where(below, scores[:, i * TILE :], neg_large)
-        if i:
-            scores = jnp.concatenate([scores[:, : i * TILE], corner], axis=1)
-        else:
-            scores = corner
-        row_max = jnp.max(scores, axis=1, keepdims=True)
-        weights = jnp.exp2((scores - row_max) * factor)
-        totals = jnp.sum(weights, axis=1, keepdims=True)
-        summed = jnp.dot(
-            weights.astype(jnp.bfloat16),
-            v_in[0 : (i + 1) * TILE, :],
-            preferred_element_type=jnp.float32,
-        )
-        attn_out[i * TILE : (i + 1) * TILE, :] = (summed / totals).astype(jnp.bfloat16)
-    attn_copies = send_back(attn_out, attn_back, 1)
+    half = rows // 2
+    halves = (half * (1 - pair), half * pair)
+    conv_copies = [
+        send_back(conv_out, conv_back, 1 + n, first, half) for n, first in enumerate(halves)
+    ]
 
     share = rows // 4
-    padded = keep.shape[1] // 2
-    order = (ch, pair_peer, core_peer, (1 - pair) * 2 + (1 - core))
+    padded = keep.shape[1]
+    chunk = keep.shape[2]
+    chunks = keep.shape[0] // 2
 
     def place(target):
-        for slot, owner in enumerate(order):
+        for slot, owner in enumerate((core, 1 - core)):
             part = stage[pl.ds(pl.multiple_of(owner * share, 8), share), :]
             filler = jnp.zeros((padded - share, width), jnp.float32)
             target[slot * padded : (slot + 1) * padded, :] = jnp.concatenate(
                 [part, filler], axis=0
             ).astype(jnp.bfloat16)
 
-    for copy in conv_copies:
-        copy.wait_recv()
-    stage[...] = qc_ref[...].astype(jnp.float32) * conv_back[...].astype(jnp.float32)
-    place(lhs_conv)
-    w1_copy.wait()
-    w2_copy.wait()
-    for copy in attn_copies:
-        copy.wait_recv()
-    stage[...] = attn_back[...].astype(jnp.float32)
-    place(lhs_attn)
-
-    chunks, unused, chunk = keep.shape
+    def take(first):
+        here = pl.ds(pl.multiple_of(first, 16), half)
+        stage[...] = qc[here, :].astype(jnp.float32) * conv_back[here, :].astype(jnp.float32)
+        place(lhs_conv)
+        stage[...] = attn_back[here, :].astype(jnp.float32)
+        place(lhs_attn)
 
     def copy_a(n):
         return pltpu.make_async_remote_copy(
@@ -432,47 +450,61 @@
             device_id_type=MESH,
         )
 
-    def project(n):
+    def project(n, base):
         cols = pl.ds(pl.multiple_of(n * chunk, chunk), chunk)
         total = jnp.dot(
             lhs_conv[...], w1[:, cols], preferred_element_type=jnp.float32
         ) + jnp.dot(lhs_attn[...], w2[:, cols], preferred_element_type=jnp.float32)
-        keep[n] = total[0 : 2 * padded]
-        send_a[n] = total[2 * padded :].astype(jnp.bfloat16)
-        copy_a(n).start()
+        keep[base + n] = total[0:padded]
+        send_a[base + n] = total[padded:].astype(jnp.bfloat16)
+        copy_a(base + n).start()
 
     def forward(n):
         copy_a(n).wait_recv()
-        send_b[n] = (
-            keep[n, padded:, :] + recv_a[n, padded:, :].astype(jnp.float32)
-        ).astype(jnp.bfloat16)
+        send_b[n] = (keep[n] + recv_a[n].astype(jnp.float32)).astype(jnp.bfloat16)
         copy_b(n).start()
 
-    project(0)
-
-    def one_chunk(n, carry):
-        project(n)
+    for copy in (qc_copy, w1_copy, w2_copy):
+        copy.wait()
+    for copy in attn_copies + conv_copies[0]:
+        copy.wait_recv()
+    take(halves[0])
+    project(0, 0)
+
+    def first_half(n, carry):
+        project(n, 0)
         forward(n - 1)
         return carry
 
-    lax.fori_loop(1, chunks, one_chunk, 0)
+    lax.fori_loop(1, chunks, first_half, 0)
     forward(chunks - 1)
+    for copy in conv_copies[1]:
+        copy.wait_recv()
+    take(halves[1])
+
+    def second_half(n, carry):
+        project(n, chunks)
+        return carry
+
+    lax.fori_loop(0, chunks, second_half, 0)
 
     def finish(n, carry):
         cols = pl.ds(pl.multiple_of(n * chunk, chunk), chunk)
+        copy_a(chunks + n).wait_recv()
         copy_b(n).wait_recv()
         total = (
-            keep[n, 0:padded, :]
-            + recv_a[n, 0:padded, :].astype(jnp.float32)
+            keep[chunks + n]
+            + recv_a[chunks + n].astype(jnp.float32)
             + recv_b[n].astype(jnp.float32)
         )
         out_ref[:, cols] = total[0:share].astype(jnp.bfloat16)
         copy_a(n).wait_send()
+        copy_a(chunks + n).wait_send()
         copy_b(n).wait_send()
         return carry
 
     lax.fori_loop(0, chunks, finish, 0)
-    for copies in inbound + [conv_copies, attn_copies]:
+    for copies in inbound + conv_copies + [attn_copies]:
         for copy in copies:
             copy.wait_send()
 
@@ -484,7 +516,6 @@
     tokens = count_ctx * rows
     groups = HD // GROUP
     wide = (rows + HALF - 1) // HALF * HALF
-    filt = jnp.pad(conv_filter.T.astype(jnp.float32), ((0, 0), (0, wide - rows)))
     share = rows // 4
     padded = (share + 15) // 16 * 16
     chunk = 512
@@ -497,9 +528,13 @@
     return pl.pallas_call(
         partial(fused_kernel, count_ctx, rows, width),
         out_shape=jax.ShapeDtypeStruct((share, dout), bf16),
-        in_specs=[vmem] * 7 + [hbm] * 2,
+        in_specs=[hbm] * 3 + [vmem] + [hbm] * 5,
         out_specs=vmem,
         scratch_shapes=[
+            pltpu.VMEM((rows, width), bf16),
+            pltpu.VMEM((rows, width), bf16),
+            pltpu.VMEM((rows, width), bf16),
+            pltpu.VMEM((conv_filter.shape[1], wide), f32),
             pltpu.VMEM((rows, width), bf16),
             pltpu.VMEM((count_ctx, groups, wide), f32),
             pltpu.VMEM((tokens, HD), bf16),
@@ -513,23 +548,23 @@
             pltpu.VMEM((groups, tokens + 2 * HALF + TILE), f32),
             pltpu.VMEM((groups, tiles * GROUP, TILE), bf16),
             pltpu.VMEM((groups, tiles * GROUP, TILE), f32),
-            pltpu.VMEM((rows, width), f32),
-            pltpu.VMEM((4 * padded, width), bf16),
-            pltpu.VMEM((4 * padded, width), bf16),
+            pltpu.VMEM((rows // 2, width), f32),
+            pltpu.VMEM((2 * padded, width), bf16),
+            pltpu.VMEM((2 * padded, width), bf16),
             pltpu.VMEM(w_conv_out.shape, bf16),
             pltpu.VMEM(w_attn_out.shape, bf16),
-            pltpu.VMEM((chunks, 2 * padded, chunk), f32),
-            pltpu.VMEM((chunks, 2 * padded, chunk), bf16),
-            pltpu.VMEM((chunks, 2 * padded, chunk), bf16),
+            pltpu.VMEM((2 * chunks, padded, chunk), f32),
+            pltpu.VMEM((2 * chunks, padded, chunk), bf16),
+            pltpu.VMEM((2 * chunks, padded, chunk), bf16),
             pltpu.VMEM((chunks, padded, chunk), bf16),
             pltpu.VMEM((chunks, padded, chunk), bf16),
             dma((5, count_ctx)),
             dma((5, count_ctx)),
-            dma((2, count_ctx)),
-            dma((2, count_ctx)),
-            dma((2,)),
-            dma((chunks,)),
-            dma((chunks,)),
+            dma((3, count_ctx)),
+            dma((3, count_ctx)),
+            dma((8,)),
+            dma((2 * chunks,)),
+            dma((2 * chunks,)),
             dma((chunks,)),
             dma((chunks,)),
         ],
@@ -537,7 +572,7 @@
             collective_id=0, has_side_effects=True, vmem_limit_bytes=56 * 1024 * 1024
         ),
         name="fused_block",
-    )(q_conv, k_conv, v_conv, filt, q_attn, k_attn, v_attn, w_conv_out, w_attn_out)
+    )(q_conv, k_conv, v_conv, conv_filter.T, q_attn, k_attn, v_attn, w_conv_out, w_attn_out)
 
 
 def local(q_conv, k_conv, v_conv, conv_filter, q_attn, k_attn, v_attn, w_conv_out, w_attn_out):

time: 88.3 us -> 84.2 us (0.954); the launches traced: 86.8 us -> 84 us
  Pallas kernels: 83.6 us -> 82.2 us
  other arithmetic: 1.39 us -> 0 us
    pad x1 -> x0, other arithmetic: 1.39 us -> none  [local_fused(): jnp.pad(conv_filter.T.astype(jnp.float32), ((0, 0), (0, wide - rows)))]
    pallas_call x1, Pallas kernels: 83.6 us -> 82.2 us  [local_fused(): pl.pallas_call(partial(fused_kernel, count_ctx, rows, width), out_shape=j...]
where the time goes in v1:
time: 84.2 us; the launch traced here: 84 us
  Pallas kernels  82.2 us (98%)
  local copies, waits for them, and re-layouts  1.82 us (2%)
    pallas_call x1, Pallas kernels, local_fused(): pl.pallas_call(partial(fused_kernel, count_ctx, rows, width), out_shape=j...  82.2 us
    unnamed x1, local copies, waits for them, and re-layouts  1.82 us

profile of v1, /device:TPU:0, one launch (start us, length us, event | category | flops | bytes accessed | tf_op | source)
XLA Modules:
  0.0 84.0 jit_solution(6266560450211027385)
XLA Ops:
  0.0 82.2 %fused_block.1 = bf16[56,4096]{1,0:T(8,128)(2,1)} custom-call(bf16[224,1024]{1,0:T(8,128)(2,1)} %qc_hbm.1, bf16[224,1024]{1,0:T(8,128)(2,1)} %kc_hbm.1, bf16[224,1024]{1,0:T(8,128)(2,1)} %vc_hbm.1, bf16[64,224]{1,0:T(8,128)(2,1)} %bitcast.1, bf16[224,1024]{1,0:T(8,128)(2,1)} %q_ref.1, bf16[224,1024]{1,0:T(8,128)(2,1)} %k_ref.1, bf16[224,1024]{1,0:T(8,128)(2,1)} %v_ref.1, ...), custom_call_target="tpu_custom_call" | custom-call | tf_op jit(solution)/shard_map/fused_block/pallas_call | solution.py:528
  82.2 1.8 %copy.11 = bf16[56,4096]{1,0:T(8,128)(2,1)} copy(bf16[56,4096]{1,0:T(8,128)(2,1)} %fused_block.1) | data formatting | bytes 917504

commit v2 on v1

--- a/solution.py
+++ b/solution.py
@@ -219,7 +219,7 @@
     out_ref,
     qc, kc, vc, filt,
     gated, filt_in, gated_in, q_in, k_in, v_in, conv_out, attn_out, conv_back, attn_back,
-    fpad, x_turned, y_turned, stage, lhs_conv, lhs_attn, w1, w2,
+    fpad, x_turned, y_turned, stage, lhs_conv, lhs_attn, attn_part, w1, w2,
     keep, send_a, recv_a, send_b, recv_b,
     in_send, in_recv, back_send, back_recv, load_sem, a_send, a_recv, b_send, b_recv,
 ):
@@ -415,20 +415,18 @@
     chunk = keep.shape[2]
     chunks = keep.shape[0] // 2
 
-    def place(target):
+    def place(target, base):
         for slot, owner in enumerate((core, 1 - core)):
             part = stage[pl.ds(pl.multiple_of(owner * share, 8), share), :]
             filler = jnp.zeros((padded - share, width), jnp.float32)
-            target[slot * padded : (slot + 1) * padded, :] = jnp.concatenate(
+            target[base + slot * padded : base + (slot + 1) * padded, :] = jnp.concatenate(
                 [part, filler], axis=0
             ).astype(jnp.bfloat16)
 
     def take(first):
         here = pl.ds(pl.multiple_of(first, 16), half)
         stage[...] = qc[here, :].astype(jnp.float32) * conv_back[here, :].astype(jnp.float32)
-        place(lhs_conv)
-        stage[...] = attn_back[here, :].astype(jnp.float32)
-        place(lhs_attn)
+        place(lhs_conv, 0)
 
     def copy_a(n):
         return pltpu.make_async_remote_copy(
@@ -450,11 +448,18 @@
             device_id_type=MESH,
         )
 
+    def project_attn(n, carry):
+        cols = pl.ds(pl.multiple_of(n * chunk, chunk), chunk)
+        attn_part[n] = jnp.dot(lhs_attn[...], w2[:, cols], preferred_element_type=jnp.float32)
+        return carry
+
     def project(n, base):
         cols = pl.ds(pl.multiple_of(n * chunk, chunk), chunk)
-        total = jnp.dot(
-            lhs_conv[...], w1[:, cols], preferred_element_type=jnp.float32
-        ) + jnp.dot(lhs_attn[...], w2[:, cols], preferred_element_type=jnp.float32)
+        row = 2 * padded if base else 0
+        total = (
+            jnp.dot(lhs_conv[...], w1[:, cols], preferred_element_type=jnp.float32)
+            + attn_part[n, row : row + 2 * padded, :]
+        )
         keep[base + n] = total[0:padded]
         send_a[base + n] = total[padded:].astype(jnp.bfloat16)
         copy_a(base + n).start()
@@ -466,7 +471,13 @@
 
     for copy in (qc_copy, w1_copy, w2_copy):
         copy.wait()
-    for copy in attn_copies + conv_copies[0]:
+    for copy in attn_copies:
+        copy.wait_recv()
+    for n, first in enumerate(halves):
+        stage[...] = attn_back[pl.ds(pl.multiple_of(first, 16), half), :].astype(jnp.float32)
+        place(lhs_attn, 2 * n * padded)
+    lax.fori_loop(0, chunks, project_attn, 0)
+    for copy in conv_copies[0]:
         copy.wait_recv()
     take(halves[0])
     project(0, 0)
@@ -550,7 +561,8 @@
             pltpu.VMEM((groups, tiles * GROUP, TILE), f32),
             pltpu.VMEM((rows // 2, width), f32),
             pltpu.VMEM((2 * padded, width), bf16),
-            pltpu.VMEM((2 * padded, width), bf16),
+            pltpu.VMEM((4 * padded, width), bf16),
+            pltpu.VMEM((chunks, 4 * padded, chunk), f32),
             pltpu.VMEM(w_conv_out.shape, bf16),
             pltpu.VMEM(w_attn_out.shape, bf16),
             pltpu.VMEM((2 * chunks, padded, chunk), f32),

time: 84.2 us -> 84.9 us (level); the launches traced: 84 us -> 83.5 us
  no operation moved by 1% of the time
where the time goes in v2:
time: 84.9 us; the launch traced here: 83.5 us
  Pallas kernels  81.7 us (96%)
  local copies, waits for them, and re-layouts  1.82 us (2%)
    pallas_call x1, Pallas kernels, local_fused(): pl.pallas_call(partial(fused_kernel, count_ctx, rows, width), out_shape=j...  81.7 us
    unnamed x1, local copies, waits for them, and re-layouts  1.82 us

profile of v2, /device:TPU:0, one launch (start us, length us, event | category | flops | bytes accessed | tf_op | source)
XLA Modules:
  0.0 83.5 jit_solution(16265848875134092622)
XLA Ops:
  0.0 81.7 %fused_block.1 = bf16[56,4096]{1,0:T(8,128)(2,1)} custom-call(bf16[224,1024]{1,0:T(8,128)(2,1)} %qc_hbm.1, bf16[224,1024]{1,0:T(8,128)(2,1)} %kc_hbm.1, bf16[224,1024]{1,0:T(8,128)(2,1)} %vc_hbm.1, bf16[64,224]{1,0:T(8,128)(2,1)} %bitcast.1, bf16[224,1024]{1,0:T(8,128)(2,1)} %q_ref.1, bf16[224,1024]{1,0:T(8,128)(2,1)} %k_ref.1, bf16[224,1024]{1,0:T(8,128)(2,1)} %v_ref.1, ...), custom_call_target="tpu_custom_call" | custom-call | tf_op jit(solution)/shard_map/fused_block/pallas_call | solution.py:539
  81.7 1.8 %copy.11 = bf16[56,4096]{1,0:T(8,128)(2,1)} copy(bf16[56,4096]{1,0:T(8,128)(2,1)} %fused_block.1) | data formatting | bytes 917504

commit v3 on v1

--- a/solution.py
+++ b/solution.py
@@ -351,7 +351,9 @@
             preferred_element_type=jnp.float32,
         )
         attn_out[i * TILE : (i + 1) * TILE, :] = (summed / totals).astype(jnp.bfloat16)
-    attn_copies = send_back(attn_out, attn_back, 0, 0, rows)
+    half = rows // 2
+    halves = (half * (1 - pair), half * pair)
+    early_copies = send_back(attn_out, attn_back, 0, halves[0], half)
 
     for copy in inbound[4]:
         copy.wait_recv()
@@ -404,11 +406,9 @@
     for i in range(tiles):
         gathered = y_turned[:, i * GROUP : (i + 1) * GROUP, :].reshape(HD, TILE)
         conv_out[i * TILE : (i + 1) * TILE, :] = gathered.T.astype(jnp.bfloat16)
-    half = rows // 2
-    halves = (half * (1 - pair), half * pair)
-    conv_copies = [
-        send_back(conv_out, conv_back, 1 + n, first, half) for n, first in enumerate(halves)
-    ]
+    early_copies += send_back(conv_out, conv_back, 1, halves[0], half)
+    late_copies = send_back(attn_out, attn_back, 2, halves[1], half)
+    late_copies += send_back(conv_out, conv_back, 3, halves[1], half)
 
     share = rows // 4
     padded = keep.shape[1]
@@ -466,7 +466,7 @@
 
     for copy in (qc_copy, w1_copy, w2_copy):
         copy.wait()
-    for copy in attn_copies + conv_copies[0]:
+    for copy in early_copies:
         copy.wait_recv()
     take(halves[0])
     project(0, 0)
@@ -478,7 +478,7 @@
 
     lax.fori_loop(1, chunks, first_half, 0)
     forward(chunks - 1)
-    for copy in conv_copies[1]:
+    for copy in late_copies:
         copy.wait_recv()
     take(halves[1])
 
@@ -504,7 +504,7 @@
         return carry
 
     lax.fori_loop(0, chunks, finish, 0)
-    for copies in inbound + conv_copies + [attn_copies]:
+    for copies in inbound + [early_copies, late_copies]:
         for copy in copies:
             copy.wait_send()
 
@@ -560,8 +560,8 @@
             pltpu.VMEM((chunks, padded, chunk), bf16),
             dma((5, count_ctx)),
             dma((5, count_ctx)),
-            dma((3, count_ctx)),
-            dma((3, count_ctx)),
+            dma((4, count_ctx)),
+            dma((4, count_ctx)),
             dma((8,)),
             dma((2 * chunks,)),
             dma((2 * chunks,)),

time: 84.2 us -> 82.5 us (0.980)
  Pallas kernels: 82.2 us -> 80.5 us
    pallas_call x1, Pallas kernels: 82.2 us -> 80.5 us  [local_fused(): pl.pallas_call(partial(fused_kernel, count_ctx, rows, width), out_shape=j...]
where the time goes in v3:
time: 82.5 us; the launch traced here: 82.3 us
  Pallas kernels  80.5 us (98%)
  local copies, waits for them, and re-layouts  1.82 us (2%)
    pallas_call x1, Pallas kernels, local_fused(): pl.pallas_call(partial(fused_kernel, count_ctx, rows, width), out_shape=j...  80.5 us
    unnamed x1, local copies, waits for them, and re-layouts  1.82 us

profile of v3, /device:TPU:0, one launch (start us, length us, event | category | flops | bytes accessed | tf_op | source)
XLA Modules:
  0.0 82.3 jit_solution(3552125434903921924)
XLA Ops:
  0.0 80.5 %fused_block.1 = bf16[56,4096]{1,0:T(8,128)(2,1)} custom-call(bf16[224,1024]{1,0:T(8,128)(2,1)} %qc_hbm.1, bf16[224,1024]{1,0:T(8,128)(2,1)} %kc_hbm.1, bf16[224,1024]{1,0:T(8,128)(2,1)} %vc_hbm.1, bf16[64,224]{1,0:T(8,128)(2,1)} %bitcast.1, bf16[224,1024]{1,0:T(8,128)(2,1)} %q_ref.1, bf16[224,1024]{1,0:T(8,128)(2,1)} %k_ref.1, bf16[224,1024]{1,0:T(8,128)(2,1)} %v_ref.1, ...), custom_call_target="tpu_custom_call" | custom-call | tf_op jit(solution)/shard_map/fused_block/pallas_call | solution.py:528
  80.5 1.8 %copy.11 = bf16[56,4096]{1,0:T(8,128)(2,1)} copy(bf16[56,4096]{1,0:T(8,128)(2,1)} %fused_block.1) | data formatting | bytes 917504
